TPU v7x, 256 devices: a whole 4x4x8 slice. The times are simulated.
256 devices in a mesh: sec: 2 (over z_hi), grp: 8 (over y, core), rank: 16 (over x, z_lo).
Axes of the slice: x: 4, y: 4, z: 8 (z_hi: 2, z_lo: 4; z = z_hi * 4 + z_lo), core: 2. Of those that a mesh axis runs over, the one named last changes fastest.
Arguments:
- queries: bfloat16 [16, 128, 8192], P(('sec', 'grp')), may hold values from -6 to 14
- kv_cache: bfloat16 [16, 16384, 2048], P(('sec', 'grp'), 'rank'), may hold values from -6 to 10
- key_scale: float32 [1024], replicated, may hold values from 0.5 to 2
- fresh_input: bfloat16 [16, 128, 8192], P(('sec', 'grp'), None, 'rank'), may hold values from -6 to 6
- kv_weight: bfloat16 [8192, 2048], P('rank'), may hold values from -0.0625 to 0.0625
- lengths: int32 [16, 1], P(('sec', 'grp')), may hold values from 1 to 16384
- page_list: int32 [4096], P(('sec', 'grp', 'rank')), may hold values from 0 to 63, as said below
- owners: int32 [4096, 1], P(('sec', 'grp', 'rank')), may hold values from 0 to 15; in each aligned block of 16 rows (0 to 15, 16 to 31, ...) at most 2 rows name the same one
Outputs:
- attended: bfloat16 [16, 128, 8192], P(('sec', 'grp'), None, 'rank')
- handed: bfloat16 [256, 32, 16, 2048], P(('sec', 'grp', 'rank'))
Inputs may be any that keep to these rules, and one draw needn't show every extreme that they name: `page_list`: the 16 entries of one device are distinct page numbers of its own cache. `owners`: among the 16 entries of one device at most 2 name the same owner, and some device has exactly 2 for one owner.
All inputs are finite; a program needn't handle non-finite values.
Results may differ from a plain program's by a relative error of at most 0.0045.
The roundings to bfloat16 on the way count: a program that leaves them out, or rounds other values in their place, can miss the bound.
Values may be sent and summed in bfloat16 or wider, within the bound.
A program may use at most 192 MiB of HBM per device.

v0:
```python
import math

import jax
import jax.numpy as jnp
from jax import lax
from jax.sharding import PartitionSpec as P

HEADS = 64
KVH = 8
HD = 128
ROWS = 128
CTX = 1024
PAGE = 16
GQ = 8
KVW = 1024


ROPE_BASE = 500000.0
NEG_FILL = -1e30


def passed_along(value, axis, by):
    devices = lax.axis_size(axis)
    pairs = [(i, i + by) for i in range(devices) if 0 <= i + by < devices]
    return lax.ppermute(value, axis, pairs)


def combined_all(part, axis, combine):
    gathered = jax.tree.map(lambda a: lax.all_gather(a, axis), part)

    def take(source):
        return jax.tree.map(lambda a: lax.dynamic_index_in_dim(a, source, 0, False), gathered)

    return lax.fori_loop(
        1, lax.axis_size(axis), lambda source, state: combine(state, take(source)), take(0)
    )


def rope_tables(positions):
    half_width = HD // 2
    steps_index = jnp.arange(half_width, dtype=jnp.float32)
    inverse = jnp.exp(steps_index * (-2.0 * math.log(ROPE_BASE) / HD))
    angles = positions.astype(jnp.float32)[:, None] * inverse[None, :]
    return (jnp.cos(angles)[:, None, :], jnp.sin(angles)[:, None, :])


def rotate_heads(values, cosine, sine_part):
    half_width = HD // 2
    first_half = values[..., :half_width]
    second_half = values[..., half_width:]
    return jnp.concatenate(
        [
            first_half * cosine - second_half * sine_part,
            second_half * cosine + first_half * sine_part,
        ],
        axis=-1,
    )


def combine_parts(earlier, latter):
    row_top = jnp.maximum(earlier[0], latter[0])
    first_factor = jnp.exp(earlier[0] - row_top)
    second_factor = jnp.exp(latter[0] - row_top)
    return (
        row_top,
        earlier[1] * first_factor + latter[1] * second_factor,
        earlier[2] * first_factor[..., None] + latter[2] * second_factor[..., None],
    )


def shards(queries, kv_cache, key_scale, fresh_input, kv_weight, lengths, page_list, owners):
    rank_count = lax.axis_size("rank")
    position = lax.axis_index("rank")
    row_share = ROWS // rank_count
    heads_here = HEADS // rank_count
    cache_rows = kv_cache[0]
    entries = page_list.shape[0]
    slot_count = 2 * entries // rank_count
    page_blocks = cache_rows.reshape(CTX // PAGE, PAGE, 2 * KVW)
    owner_ids = owners[:, 0]
    targets = jnp.arange(rank_count, dtype=jnp.int32)
    onehot = (owner_ids[:, None] == targets[None, :]).astype(jnp.int32)
    running = jnp.cumsum(onehot, axis=0)
    slot_index = jnp.sum(onehot * running, axis=1) - 1
    places = jnp.arange(slot_count, dtype=jnp.int32)
    matches = (owner_ids[None, None, :] == targets[:, None, None]) & (
        slot_index[None, None, :] == places[None, :, None]
    )
    present = jnp.any(matches, axis=-1)
    chosen = jnp.sum(jnp.where(matches, page_list[None, None, :], 0), axis=-1)
    outgoing = jnp.where(present[..., None, None], page_blocks[chosen], jnp.zeros((), jnp.bfloat16))
    routed = lax.all_to_all(outgoing, "rank", split_axis=0, concat_axis=0, tiled=True)
    handed = passed_along(routed, "sec", 1)
    handed = handed.reshape(1, rank_count * slot_count, PAGE, 2 * KVW)
    rows_in = fresh_input[0]
    summed = lax.psum(jnp.dot(rows_in, kv_weight, preferred_element_type=jnp.float32), "rank")
    fresh_sum = lax.dynamic_slice_in_dim(summed, position * row_share, row_share, 0)
    fresh_kv = fresh_sum.astype(jnp.bfloat16)
    length = lengths[0, 0]
    row_ids = jnp.arange(ROWS, dtype=jnp.int32)
    cosine, sine_part = rope_tables(length + row_ids)
    query_rot = rotate_heads(
        queries[0].astype(jnp.float32).reshape(ROWS, HEADS, HD), cosine, sine_part
    ).astype(jnp.bfloat16)
    fresh_ids = position * row_share + jnp.arange(row_share, dtype=jnp.int32)
    fresh_cos, fresh_sin = rope_tables(length + fresh_ids)
    fresh_keys = rotate_heads(
        fresh_kv[:, :KVW].astype(jnp.float32).reshape(row_share, KVH, HD), fresh_cos, fresh_sin
    ).astype(jnp.bfloat16)
    cache_pos = position * CTX + jnp.arange(CTX, dtype=jnp.int32)
    cache_cos, cache_sin = rope_tables(cache_pos)
    scaled = (cache_rows[:, :KVW].astype(jnp.float32) * key_scale[None, :]).reshape(CTX, KVH, HD)
    cache_keys = rotate_heads(scaled, cache_cos, cache_sin).astype(jnp.bfloat16)
    keys_all = jnp.concatenate([cache_keys, fresh_keys], axis=0).transpose(1, 0, 2)
    vals_all = jnp.concatenate(
        [cache_rows[:, KVW:].reshape(CTX, KVH, HD), fresh_kv[:, KVW:].reshape(row_share, KVH, HD)],
        axis=0,
    ).transpose(1, 0, 2)
    allowed = jnp.concatenate(
        [
            jnp.broadcast_to((cache_pos < length)[None, :], (ROWS, CTX)),
            fresh_ids[None, :] <= row_ids[:, None],
        ],
        axis=1,
    )
    allowed_rows = jnp.repeat(allowed, GQ, axis=0)
    query_groups = (
        query_rot.reshape(ROWS, KVH, GQ, HD).transpose(1, 0, 2, 3).reshape(KVH, ROWS * GQ, HD)
    )

    def per_head(head_item):
        query_head, key_head, value_head = head_item
        scores = jnp.dot(query_head, key_head.T, preferred_element_type=jnp.float32) / math.sqrt(HD)
        masked = jnp.where(allowed_rows, scores, NEG_FILL)
        row_peak = jnp.max(masked, axis=-1)
        weights = jnp.where(allowed_rows, jnp.exp(masked - row_peak[:, None]), 0.0)
        row_total = jnp.sum(weights, axis=-1)
        numerator = jnp.dot(
            weights.astype(jnp.bfloat16), value_head, preferred_element_type=jnp.float32
        )
        return (row_peak, row_total, numerator)

    peaks, totals, numerators = lax.map(per_head, (query_groups, keys_all, vals_all))
    peaks = peaks.reshape(KVH, ROWS, GQ).transpose(1, 0, 2).reshape(ROWS, HEADS)
    totals = totals.reshape(KVH, ROWS, GQ).transpose(1, 0, 2).reshape(ROWS, HEADS)
    numerators = (
        numerators.reshape(KVH, ROWS, GQ, HD).transpose(1, 0, 2, 3).reshape(ROWS, HEADS, HD)
    )
    merged = combined_all((peaks, totals, numerators), "rank", combine_parts)
    own_numerator = lax.dynamic_slice_in_dim(merged[2], position * heads_here, heads_here, 1)
    own_total = lax.dynamic_slice_in_dim(merged[1], position * heads_here, heads_here, 1)
    attended = (
        (own_numerator / own_total[..., None])
        .reshape(1, ROWS, heads_here * HD)
        .astype(jnp.bfloat16)
    )
    return (attended, handed)


def solution(mesh):
    return jax.shard_map(
        shards,
        mesh=mesh,
        in_specs=(
            P(("sec", "grp"), None, None),
            P(("sec", "grp"), "rank", None),
            P(),
            P(("sec", "grp"), None, "rank"),
            P("rank", None),
            P(("sec", "grp"), None),
            P(("sec", "grp", "rank")),
            P(("sec", "grp", "rank"), None),
        ),
        out_specs=(P(("sec", "grp"), None, "rank"), P(("sec", "grp", "rank"), None, None, None)),
        check_vma=False,
    )
```

profile of v0, /device:TPU:1, one launch (start us, length us, event | category | flops | bytes accessed | tf_op | source)
XLA Modules:
  0.0 1858.3 jit_solution(10142925305641338672)
XLA Ops:
  10.1 90.6 %all-reduce.1 = bf16[128,2048]{1,0:T(8,128)(2,1)S(1)} all-reduce(f32[128,2048]{1,0:T(8,128)S(1)} %fusion.28), channel_id=1, replica_groups=mesh['sec'=2,'grp'=8,'rank'=16] {'rank'}, use_global_device_ids=true, to_apply=%region_0.0 | all-reduce | flops 262144 | bytes 1572864 | tf_op jit(solution)/shard_map/psum | solution.py:96
  102.9 6.5 copy.72
  114.9 4.2 copy.77
  119.3 4.3 copy.70
  123.7 2.8 subtract_convert_fusion.1
  128.0 4.1 copy.71
  133.9 4.2 copy.78
  138.3 68.9 %while.35 = (s32[]{:T(128)}, f32[8,1024]{1,0:T(8,128)S(1)}, f32[8,1024]{1,0:T(8,128)S(1)}, f32[8,1024,128]{2,1,0:T(8,128)}, bf16[8,1024,128]{2,1,0:T(8,128)(2,1)...) while((s32[]{:T(128)}, f32[8,1024]{1,0:T(8,128)S(1)}, ...), condition=%wide.region_4.5_spmd.clone, body=%wide.region_1.0_spmd.clone.sunk | while | flops 550574080 | bytes 20503660 | solution.py:143
  140.7 1.9 fusion.51
  142.7 2.9 fusion.53
  149.3 1.9 fusion.51
  151.3 3.0 fusion.53
  157.9 2.0 fusion.51
  159.9 3.0 fusion.53
  168.5 2.9 fusion.53
  175.2 1.9 fusion.51
  177.1 2.9 fusion.53
  183.8 2.0 fusion.51
  185.7 3.0 fusion.53
  192.4 2.0 fusion.51
  194.4 3.0 fusion.53
  201.0 1.9 fusion.51
  203.0 3.0 fusion.53
  207.2 4.7 copy_bitcast_fusion
  213.5 2.9 gather_fusion
  216.6 84.6 %all_to_all.5 = bf16[16,2,16,2048]{3,2,1,0:T(8,128)(2,1)} all-to-all(bf16[16,2,16,2048]{3,2,1,0:T(8,128)(2,1)S(1)} %broadcast_select_fusion), channel_id=1, replica_groups=mesh['sec'=2,'grp'=8,'rank'=16] {'rank'}, dimensions={0} | all-to-all | bytes 4194304 | tf_op jit(solution)/shard_map/all_to_all | solution.py:92
  301.2 6.4 collective-permute-start
  308.0 261.6 %all_gather.9 = f32[16,128,64]{1,2,0:T(8,128)S(1)} all-gather(f32[1,128,64]{1,2,0:T(8,128)S(1)} %bitcast.122), channel_id=1, replica_groups=mesh['sec'=2,'grp'=8,'rank'=16] {'rank'}, dimensions={0}, use_global_device_ids=true | all-gather | bytes 557056 | tf_op jit(solution)/shard_map/all_gather | solution.py:29
  570.2 60.7 %all_gather.10 = f32[16,128,64]{1,2,0:T(8,128)S(1)} all-gather(f32[1,128,64]{1,2,0:T(8,128)S(1)} %bitcast.123), channel_id=1, replica_groups=mesh['sec'=2,'grp'=8,'rank'=16] {'rank'}, dimensions={0}, use_global_device_ids=true | all-gather | bytes 557056 | tf_op jit(solution)/shard_map/all_gather | solution.py:29
  631.0 1086.4 %all-gather.2.cloned.1.call-done = f32[16,128,64,128]{3,2,1,0:T(8,128)} async-done(((f32[1,128,64,128]{3,2,1,0:T(8,128)}), f32[16,128,64,128]{3,2,1,0:T(8,128)}) %all-gather.2.cloned.1.call-update) | async-done | bytes 67108880 | tf_op jit(solution)/shard_map/all_gather | solution.py:29
  1717.4 4.8 slice_bitcast_fusion
  1722.1 123.9 %while.34 = (s32[]{:T(128)}, f32[128,64]{1,0:T(8,128)S(1)}, f32[128,64]{1,0:T(8,128)S(1)}, f32[128,64,128]{2,1,0:T(8,128)}, f32[16,128,64]{1,2,0:T(8,128)S(1)}, ...) while((s32[]{:T(128)}, f32[128,64]{1,0:T(8,128)S(1)}, ...), condition=%wide.region_6.7_spmd, body=%wide.region_5.6_spmd.sunk | while | flops 3194885 | bytes 13172887 | solution.py:34
  1722.4 8.0 fusion.48
  1730.7 8.0 fusion.48
  1739.0 8.0 fusion.48
  1747.2 8.0 fusion.48
  1755.5 8.0 fusion.48
  1763.7 8.0 fusion.48
  1772.0 8.0 fusion.48
  1780.3 8.0 fusion.48
  1788.5 8.0 fusion.48
  1796.8 8.0 fusion.48
  1805.1 8.0 fusion.48
  1813.3 8.0 fusion.48
  1821.6 8.0 fusion.48
  1829.8 8.0 fusion.48
  1838.1 8.0 fusion.48
  1848.3 3.2 copy.134
  (170 shorter events, 53.6 us)
Async XLA Ops:
  7.2 1.6 copy-start
  7.2 1710.2 %all-gather.2.cloned.1.call-start = ((), (), s32[]{:S(2)}) async-start(), calls=%async_computation.1 | async-start | bytes 71303168 | tf_op jit(solution)/shard_map/all_gather | solution.py:29
  102.9 8.4 copy-start.5
  109.4 2.8 copy-start.2
  212.0 0.7 copy-start.4
  212.0 1.0 copy-start.6
  301.2 329.8 %collective-permute-start = (bf16[16,2,16,2048]{3,2,1,0:T(8,128)(2,1)}, bf16[16,2,16,2048]{3,2,1,0:T(8,128)(2,1)S(1)}, u32[]{:S(2)}, u32[]{:S(2)}) collective-permute-start(bf16[16,2,16,2048]{3,2,1,0:T(8,128)(2,1)} %all_to_all.5), channel_id=1, source_target_pairs={{0,128},{1,129},{2,130},{3,131},{4,132},{5,133},{6,134},{7,135},{8... | collective-permute-start | bytes 6291464 | tf_op jit(solution)/shard_map/ppermute | solution.py:25
  631.0 1091.1 %copy-start.3 = (bf16[16,2,16,2048]{3,2,1,0:T(8,128)(2,1)}, bf16[16,2,16,2048]{3,2,1,0:T(8,128)(2,1)S(1)}, u32[]{:S(2)}) copy-start(bf16[16,2,16,2048]{3,2,1,0:T(8,128)(2,1)S(1)} %collective-permute-done) | copy-start | bytes 6291460
  1846.1 5.4 copy-start.1
Sparse Core Ops, SparseCore 0:
  212.1 1505.2 all-gather.1
where the time goes:
time: 1860 us
  waiting for transfers between devices  1090 us (59%)
  blocking collectives  497 us (27%)
  other arithmetic  142 us (8%)
  local copies, waits for them, and re-layouts  70.1 us (4%)
  matrix products  40.6 us (2%)
    all_gather x1, waiting for transfers between devices, combined_all(): gathered = jax.tree.map(lambda a: lax.all_gather(a, axis), part)  1090 us
    all_gather x2, blocking collectives, combined_all(): gathered = jax.tree.map(lambda a: lax.all_gather(a, axis), part)  322 us
    add x15, other arithmetic, combine_parts(): earlier[2] * first_factor[..., None] + latter[2] * second_factor[..., None]  120 us
    psum x1, blocking collectives, shards(): lax.psum(jnp.dot(rows_in, kv_weight, preferred_element_type=jnp.float32),...  90.6 us
    all_to_all x1, blocking collectives, shards(): lax.all_to_all(outgoing, 'rank', split_axis=0, concat_axis=0, tiled=True)  84.6 us
  transfers between devices with their start and end apart: 2, of which 1 were waited for; matrix products, arithmetic and copies ran while one was open for 0% of the time, Pallas kernels for 0%

commit v1 on v0

v1 whole, which is shorter than its diff:
```python
import functools
import math

import jax
import jax.numpy as jnp
from jax import lax
from jax.experimental import pallas as pl
from jax.experimental.pallas import tpu as pltpu
from jax.sharding import PartitionSpec as P

HEADS = 64
KVH = 8
HD = 128
ROWS = 128
CTX = 1024
PAGE = 16
GQ = 8
KVW = 1024
PAGES = CTX // PAGE
FIN = 16
CAP = 2
NX = 4
QUARTERS = 4
QCOLS = 2 * KVW // QUARTERS
CHUNK = 4
CHUNKS = 2 * QUARTERS * FIN // CHUNK
WINDOW = 4

ROPE_BASE = 500000.0
NEG_FILL = -1e30
TO_LOG2 = math.log2(math.e) / math.sqrt(HD)

F32 = jnp.float32
BF16 = jnp.bfloat16
MESH = pl.DeviceIdType.MESH


def rope_tables(positions):
    half_width = HD // 2
    steps_index = jnp.arange(half_width, dtype=jnp.float32)
    inverse = jnp.exp(steps_index * (-2.0 * math.log(ROPE_BASE) / HD))
    angles = positions.astype(jnp.float32)[:, None] * inverse[None, :]
    cosine, sine = jnp.cos(angles), jnp.sin(angles)
    return jnp.concatenate([cosine, cosine], axis=1), jnp.concatenate([-sine, sine], axis=1)


def rotate(values, cosine, sine):
    swapped = jnp.concatenate([values[:, HD // 2 :], values[:, : HD // 2]], axis=1)
    return values * cosine + swapped * sine


def dot_nt(a, b):
    return lax.dot_general(a, b, (((1,), (1,)), ((), ())), preferred_element_type=F32)


def soft_block(scores):
    peak = jnp.max(scores, axis=0, keepdims=True)
    weights = jnp.exp2((scores - peak) * TO_LOG2)
    total = jnp.sum(weights, axis=0, keepdims=True)
    return peak * TO_LOG2, total, weights.astype(BF16)


def merge(parts):
    top = functools.reduce(jnp.maximum, [p[0] for p in parts])
    factors = [jnp.exp2(p[0] - top) for p in parts]
    total = sum(p[1] * f for p, f in zip(parts, factors))
    numerator = sum(p[2] * f for p, f in zip(parts, factors))
    return top, total, numerator


def kernel(
    q_hbm, cache_hbm, fin_hbm, w_hbm, scale_ref, ccos_ref, csin_ref, qcos_ref, qsin_ref, len_ref, plist_ref, own_ref,
    att_ref, handed_ref,
    q_ref, cache_ref, fin_ref, w_ref,
    keys, rows, vals_t,
    xs, xst, xr, xrt, zs, zst, zr, zrt,
    fs, fr, gs, gr,
    page_out, stream, work, picked, meta_out, meta_in, meta,
    load_sem, meta_send, meta_recv, meta_load, page_send, stream_send, stream_recv,
    xs_send, xs_recv, xt_send, xt_recv, zs_send, zs_recv, zt_send, zt_recv,
    f_send, f_recv, g_send, g_recv, pick_send, pick_recv, own_sem,
):
    sec, grp, rank = lax.axis_index("sec"), lax.axis_index("grp"), lax.axis_index("rank")
    x, z = lax.div(rank, NX), lax.rem(rank, NX)

    def at(xx, zz, section=None):
        return (sec if section is None else section, grp, xx * NX + zz)

    def remote(src, dst, send, recv, device):
        return pltpu.make_async_remote_copy(
            src_ref=src, dst_ref=dst, send_sem=send, recv_sem=recv, device_id=device, device_id_type=MESH
        )

    def plus(value, by):
        return lax.rem(value + by, NX)

    loads = [
        pltpu.make_async_copy(src, dst, load_sem.at[i])
        for i, (src, dst) in enumerate(
            ((cache_hbm, cache_ref), (fin_hbm, fin_ref), (w_hbm, w_ref), (q_hbm, q_ref))
        )
    ]
    for load in loads:
        load.start()

    barrier = pltpu.get_barrier_semaphore()
    for o in range(1, NX):
        pl.semaphore_signal(barrier, inc=1, device_id=at(plus(x, o), z), device_id_type=MESH)
        pl.semaphore_signal(barrier, inc=1, device_id=at(x, plus(z, o)), device_id_type=MESH)
    for zz in range(NX):
        pl.semaphore_signal(barrier, inc=1, device_id=at(x, zz, 1 - sec), device_id_type=MESH)

    rightward = z >= NX // 2
    entry = jnp.where(rightward, 0, NX - 1)
    lane = jnp.where(rightward, 0, 1)
    nearness = jnp.where(rightward, NX - 1 - z, z)

    def page_copy(m):
        n = lax.div(m, FIN // CHUNK) * (2 * FIN // CHUNK) + lax.rem(m, FIN // CHUNK) * 2 + nearness
        return remote(
            page_out.at[m], stream.at[lane, n], page_send.at[m], stream_recv.at[lane, n], at(x, entry, 1)
        )

    def meta_copy(zz):
        return remote(meta_out, meta_in.at[z], meta_send.at[zz], meta_recv.at[z], at(x, zz, 1))

    loads[0].wait()

    @pl.when(sec == 0)
    def _():
        lanes = lax.broadcasted_iota(jnp.int32, (8, 128), 1)
        owner_of, slot_of = lanes // CAP, lanes % CAP
        count = jnp.zeros((8, 128), jnp.int32)
        chosen = jnp.full((8, 128), FIN, jnp.int32)
        for f in range(FIN):
            mine = owner_of == own_ref[f]
            chosen = jnp.where(mine & (count == slot_of), f, chosen)
            count = count + jnp.where(mine, 1, 0)
        meta_out[...] = chosen

        @pl.loop(0, FIN)
        def _(f):
            page = plist_ref[f]
            for part in range(QUARTERS):
                page_out[part * (FIN // CHUNK) + lax.div(f, CHUNK), lax.rem(f, CHUNK)] = cache_ref[
                    page, :, part * QCOLS : (part + 1) * QCOLS
                ]

    pl.semaphore_wait(barrier, 2 * (NX - 1) + NX)

    @pl.when(sec == 0)
    def _():
        for zz in range(NX):
            meta_copy(zz).start()
        for m in range(WINDOW):
            page_copy(m).start()

    loads[1].wait()
    loads[2].wait()

    def fresh_x(xx):
        o = plus(xx - x + NX, 0)
        return remote(fs.at[xx], fr.at[o], f_send.at[o], f_recv.at[o], at(xx, z))

    for xx in range(NX):
        for kind in range(2):
            cols = slice(kind * KVW + xx * 2 * HD, kind * KVW + (xx + 1) * 2 * HD)
            fs[xx, kind] = jnp.dot(fin_ref[...], w_ref[:, cols], preferred_element_type=F32)

        @pl.when(xx != x)
        def _():
            fresh_x(xx).start()

    def fresh_z(zz):
        o = plus(zz - z + NX, 0)
        return remote(gs.at[zz // 2], gr.at[o], g_send.at[o], g_recv.at[o], at(x, zz))

    def fresh_sum_x():
        for o in range(1, NX):
            remote(fs.at[0], fr.at[o], f_send.at[o], f_recv.at[o], at(plus(x, o), z)).wait_recv()
        for kind in range(2):
            total = fs[x, kind] + fr[1, kind] + fr[2, kind] + fr[3, kind]
            gs[0, kind] = total[:, :HD]
            gs[1, kind] = total[:, HD:]
        for zz in range(NX):

            @pl.when(zz != z)
            def _():
                fresh_z(zz).start()

    def stream_copy(d, n):
        onward = jnp.minimum(z + 1, NX - 1) if d == 0 else jnp.maximum(z - 1, 0)
        return remote(
            stream.at[d, n], stream.at[d, n], stream_send.at[d, n], stream_recv.at[d, n], at(x, onward, 1)
        )

    def stream_step(n):
        for d in range(2):
            stream_copy(d, n).wait_recv()

            @pl.when((z < NX - 1) if d == 0 else (z > 0))
            def _():
                stream_copy(d, n).start()

    def picked_copy(part, o):
        xx = plus(x, o)
        return remote(
            picked.at[part, pl.ds(xx * 8, 8)],
            handed_ref.at[pl.ds(x * 8, 8), :, pl.ds(part * QCOLS, QCOLS)],
            pick_send.at[part, o],
            pick_recv.at[part, o],
            at(xx, z, 1),
        )

    def picked_own(part):
        return pltpu.make_async_copy(
            picked.at[part, pl.ds(x * 8, 8)],
            handed_ref.at[pl.ds(x * 8, 8), :, pl.ds(part * QCOLS, QCOLS)],
            own_sem.at[part],
        )

    def dispatch(part):
        for zz in range(NX):
            d, s = (0, NX - 1 - zz) if zz >= NX // 2 else (1, zz)

            @pl.loop(0, FIN)
            def _(f):
                n = part * (2 * FIN // CHUNK) + lax.div(f, CHUNK) * 2 + s
                work[zz, f] = stream[d, n, lax.rem(f, CHUNK)]

        @pl.loop(0, NX)
        def _(xx):
            for zz in range(NX):
                for c in range(CAP):
                    index = meta[zz, 0, (xx * NX + z) * CAP + c]
                    picked[part, xx * 8 + zz * CAP + c] = work[zz, index]

        for o in range(1, NX):
            picked_copy(part, o).start()
        picked_own(part).start()

    @pl.when(sec == 1)
    def _():
        for zz in range(NX):
            work[zz, FIN] = jnp.zeros((PAGE, QCOLS), BF16)

    loads[3].wait()
    edge = len_ref[0] - rank * CTX
    inside = lax.broadcasted_iota(jnp.int32, (CTX, HD), 0) < edge
    first = lax.broadcasted_iota(jnp.int32, (CTX, HD), 1) == 0
    keys[:, HD:] = jnp.where(first & jnp.logical_not(inside), NEG_FILL, 0.0).astype(BF16)
    rows[:, HD:] = jnp.where(first, 1.0, 0.0).astype(BF16)

    def xs_copy(o):
        xx = plus(x, o)
        return (
            remote(xs.at[xx], xr.at[o], xs_send.at[o], xs_recv.at[o], at(xx, z)),
            remote(xst.at[xx], xrt.at[o], xt_send.at[o], xt_recv.at[o], at(xx, z)),
        )

    @pl.loop(0, 2 * KVH)
    def _(u):
        j, half = lax.div(u, 2), lax.rem(u, 2)
        o = plus(lax.div(j, 2), 1)
        xx, hh = plus(x, o), lax.rem(j, 2)
        head = xx * 2 + hh

        @pl.when(half == 0)
        def _():
            cols = pl.ds(pl.multiple_of(head * HD, HD), HD)
            raw = cache_ref[:, :, cols].reshape(CTX, HD).astype(F32) * scale_ref[:, cols]
            keys[:, :HD] = rotate(raw, ccos_ref[...], csin_ref[...]).astype(BF16)
            val_cols = pl.ds(pl.multiple_of(KVW + head * HD, HD), HD)
            vals_t[...] = cache_ref[:, :, val_cols].reshape(CTX, HD).T
            for g in range(GQ):
                q_cols = pl.ds(pl.multiple_of((head * GQ + g) * HD, HD), HD)
                rows[g * ROWS : (g + 1) * ROWS, :HD] = rotate(
                    q_ref[:, q_cols].astype(F32), qcos_ref[...], qsin_ref[...]
                ).astype(BF16)

        for b in range(2):
            cols = pl.ds(pl.multiple_of(half * 512 + b * 256, 256), 256)
            scores = dot_nt(keys[...], rows[cols, :])
            peak, total, weights = soft_block(scores)
            numerator = jnp.dot(vals_t[...], weights, preferred_element_type=F32)
            xs[xx, hh, :, cols] = numerator.astype(BF16)
            for h in range(2):

                @pl.when(hh == h)
                def _():
                    xst[xx, 2 * h : 2 * h + 1, cols] = peak
                    xst[xx, 2 * h + 1 : 2 * h + 2, cols] = total

        @pl.when((lax.rem(u, 4) == 3) & (o != 0))
        def _():
            for copy in xs_copy(o):
                copy.start()

        @pl.when(sec == 0)
        def _():
            page_copy(u).wait_send()

            @pl.when(u + WINDOW < FIN)
            def _():
                page_copy(u + WINDOW).start()

        @pl.when(sec == 1)
        def _():
            stream_step(u)

        @pl.when(u == 8)
        def _():
            fresh_sum_x()

        @pl.when((sec == 1) & (u == 9))
        def _():
            for zz in range(NX):
                remote(meta_out, meta_in.at[zz], meta_send.at[zz], meta_recv.at[zz], at(x, zz, 0)).wait_recv()
            load = pltpu.make_async_copy(meta_in, meta, meta_load)
            load.start()
            load.wait()
            dispatch(0)

    @pl.when(sec == 0)
    def _():
        picked[0] = jnp.zeros((2 * FIN, PAGE, QCOLS), BF16)
        for part in range(QUARTERS):
            pltpu.make_async_copy(
                picked.at[0], handed_ref.at[:, :, pl.ds(part * QCOLS, QCOLS)], own_sem.at[part]
            ).start()

    @pl.when(sec == 1)
    def _():
        dispatch(1)

    for o in range(1, NX):
        for copy in xs_copy(o):
            copy.wait_recv()

    def zs_copy(zz):
        o = plus(zz - z + NX, 0)
        return (
            remote(zs.at[zz], zr.at[o], zs_send.at[o], zs_recv.at[o], at(x, zz)),
            remote(zst.at[zz], zrt.at[o], zt_send.at[o], zt_recv.at[o], at(x, zz)),
        )

    for zz in range(NX):
        hh, cols = zz // 2, slice((zz % 2) * 512, (zz % 2 + 1) * 512)
        parts = [
            (xst[x, 2 * hh : 2 * hh + 1, cols], xst[x, 2 * hh + 1 : 2 * hh + 2, cols], xs[x, hh, :, cols].astype(F32))
        ]
        for o in range(1, NX):
            parts.append(
                (
                    xrt[o, 2 * hh : 2 * hh + 1, cols],
                    xrt[o, 2 * hh + 1 : 2 * hh + 2, cols],
                    xr[o, hh, :, cols].astype(F32),
                )
            )
        top, total, numerator = merge(parts)
        zs[zz] = numerator.astype(BF16)
        zst[zz, 0:1, :] = top
        zst[zz, 1:2, :] = total

        @pl.when(zz != z)
        def _():
            for copy in zs_copy(zz):
                copy.start()

    for o in range(1, NX):
        remote(gs.at[0], gr.at[o], g_send.at[o], g_recv.at[o], at(x, plus(z, o))).wait_recv()
    mine = lax.div(z, 2)
    fresh = [(gs[mine, kind] + gr[1, kind] + gr[2, kind] + gr[3, kind]).astype(BF16) for kind in range(2)]
    fresh_keys = rotate(fresh[0].astype(F32), qcos_ref[...], qsin_ref[...]).astype(BF16)
    own_rows = []
    for h in range(HEADS // (NX * NX)):
        q_cols = pl.ds(pl.multiple_of((rank * 4 + h) * HD, HD), HD)
        own_rows.append(rotate(q_ref[:, q_cols].astype(F32), qcos_ref[...], qsin_ref[...]).astype(BF16))
    scores = dot_nt(fresh_keys, jnp.concatenate(own_rows, axis=0))
    key_row = lax.broadcasted_iota(jnp.int32, scores.shape, 0)
    query_row = lax.broadcasted_iota(jnp.int32, scores.shape, 1) % ROWS
    peak, total, weights = soft_block(jnp.where(key_row <= query_row, scores, NEG_FILL))
    numerator = jnp.dot(fresh[1].astype(F32).T.astype(BF16), weights, preferred_element_type=F32)
    parts = [(peak, total, numerator)]

    @pl.when(sec == 1)
    def _():
        @pl.loop(16, 24)
        def _(n):
            stream_step(n)

        dispatch(2)

    for o in range(1, NX):
        for copy in zs_copy(plus(z, o)):
            copy.wait_recv()
    parts.append((zst[z, 0:1, :], zst[z, 1:2, :], zs[z].astype(F32)))
    for o in range(1, NX):
        parts.append((zrt[o, 0:1, :], zrt[o, 1:2, :], zr[o].astype(F32)))
    _, total, numerator = merge(parts)
    result = numerator / total
    for h in range(HEADS // (NX * NX)):
        att_ref[0, :, h * HD : (h + 1) * HD] = result[:, h * ROWS : (h + 1) * ROWS].T.astype(BF16)

    @pl.when(sec == 1)
    def _():
        @pl.loop(24, 32)
        def _(n):
            stream_step(n)

        dispatch(3)

    for o in range(1, NX):
        for copy in xs_copy(o):
            copy.wait_send()
        for copy in zs_copy(plus(z, o)):
            copy.wait_send()
        fresh_x(plus(x, o)).wait_send()
        remote(gs.at[0], gr.at[o], g_send.at[o], g_recv.at[o], at(x, plus(z, o))).wait_send()

    @pl.when(sec == 0)
    def _():
        for zz in range(NX):
            meta_copy(zz).wait_send()
        for part in range(QUARTERS):
            pltpu.make_async_copy(
                picked.at[0], handed_ref.at[:, :, pl.ds(part * QCOLS, QCOLS)], own_sem.at[part]
            ).wait()

    @pl.when(sec == 1)
    def _():
        for d in range(2):

            @pl.when((z < NX - 1) if d == 0 else (z > 0))
            def _():
                @pl.loop(0, CHUNKS)
                def _(n):
                    stream_copy(d, n).wait_send()

        for part in range(QUARTERS):
            for o in range(1, NX):
                picked_copy(part, o).wait_send()
                picked_copy(part, o).wait_recv()
            picked_own(part).wait()


def shards(queries, kv_cache, key_scale, fresh_input, kv_weight, lengths, page_list, owners):
    position = lax.axis_index("rank")
    length = lengths[0, 0]
    qcos, qsin = rope_tables(length + jnp.arange(ROWS, dtype=jnp.int32))
    ccos, csin = rope_tables(position * CTX + jnp.arange(CTX, dtype=jnp.int32))
    whole = pl.BlockSpec(memory_space=pltpu.VMEM)
    scalars = pl.BlockSpec(memory_space=pltpu.SMEM)
    anywhere = pl.BlockSpec(memory_space=pl.ANY)
    dma = pltpu.SemaphoreType.DMA
    attended, handed = pl.pallas_call(
        kernel,
        out_shape=(
            jax.ShapeDtypeStruct((1, ROWS, 512), BF16),
            jax.ShapeDtypeStruct((2 * FIN, PAGE, 2 * KVW), BF16),
        ),
        in_specs=[anywhere] * 4 + [whole] * 5 + [scalars] * 3,
        out_specs=(whole, anywhere),
        scratch_shapes=[
            pltpu.VMEM((ROWS, HEADS * HD), BF16),
            pltpu.VMEM((PAGES, PAGE, 2 * KVW), BF16),
            pltpu.VMEM((ROWS, 512), BF16),
            pltpu.VMEM((512, 2 * KVW), BF16),
            pltpu.VMEM((CTX, 2 * HD), BF16),
            pltpu.VMEM((CTX, 2 * HD), BF16),
            pltpu.VMEM((HD, CTX), BF16),
            pltpu.VMEM((NX, 2, HD, CTX), BF16),
            pltpu.VMEM((NX, 8, CTX), F32),
            pltpu.VMEM((NX, 2, HD, CTX), BF16),
            pltpu.VMEM((NX, 8, CTX), F32),
            pltpu.VMEM((NX, HD, 512), BF16),
            pltpu.VMEM((NX, 8, 512), F32),
            pltpu.VMEM((NX, HD, 512), BF16),
            pltpu.VMEM((NX, 8, 512), F32),
            pltpu.VMEM((NX, 2, ROWS, 2 * HD), F32),
            pltpu.VMEM((NX, 2, ROWS, 2 * HD), F32),
            pltpu.VMEM((2, 2, ROWS, HD), F32),
            pltpu.VMEM((NX, 2, ROWS, HD), F32),
            pltpu.VMEM((CHUNKS // 2, CHUNK, PAGE, QCOLS), BF16),
            pltpu.VMEM((2, CHUNKS, CHUNK, PAGE, QCOLS), BF16),
            pltpu.VMEM((NX, FIN + 1, PAGE, QCOLS), BF16),
            pltpu.VMEM((QUARTERS, 2 * FIN, PAGE, QCOLS), BF16),
            pltpu.VMEM((8, 128), jnp.int32),
            pltpu.VMEM((NX, 8, 128), jnp.int32),
            pltpu.SMEM((NX, 8, 128), jnp.int32),
            dma((4,)),
            dma((NX,)),
            dma((NX,)),
            dma,
            dma((CHUNKS // 2,)),
            dma((2, CHUNKS)),
            dma((2, CHUNKS)),
        ]
        + [dma((NX,))] * 12
        + [dma((QUARTERS, NX)), dma((QUARTERS, NX)), dma((QUARTERS,))],
        compiler_params=pltpu.CompilerParams(
            collective_id=0, has_side_effects=True, vmem_limit_bytes=56 * 1024 * 1024
        ),
        cost_estimate=pl.CostEstimate(flops=4_500_000_000, bytes_accessed=12_000_000, transcendentals=8_500_000),
        name="attend_and_hand",
    )(
        queries[0],
        kv_cache.reshape(PAGES, PAGE, 2 * KVW),
        fresh_input[0],
        kv_weight,
        key_scale.reshape(1, KVW),
        ccos,
        csin,
        qcos,
        qsin,
        lengths.reshape(1),
        page_list,
        owners.reshape(FIN),
    )
    return attended, handed[None]


def solution(mesh):
    return jax.shard_map(
        shards,
        mesh=mesh,
        in_specs=(
            P(("sec", "grp"), None, None),
            P(("sec", "grp"), "rank", None),
            P(),
            P(("sec", "grp"), None, "rank"),
            P("rank", None),
            P(("sec", "grp"), None),
            P(("sec", "grp", "rank")),
            P(("sec", "grp", "rank"), None),
        ),
        out_specs=(P(("sec", "grp"), None, "rank"), P(("sec", "grp", "rank"), None, None, None)),
        check_vma=False,
    )
```

time: 1860 us -> 722 us (0.39)
  the two profiles are of different devices: /device:TPU:1 before, /device:TPU:240 now
where the time goes in v1:
time: 722 us; the launch traced here: 712 us
  Pallas kernels  702 us (97%)
    pallas_call x1, Pallas kernels, shards(): pl.pallas_call(kernel, out_shape=(jax.ShapeDtypeStruct((1, ROWS, 512), BF...  702 us

profile of v1, /device:TPU:240, one launch (start us, length us, event | category | flops | bytes accessed | tf_op | source)
XLA Modules:
  0.0 712.0 jit_solution(10094709984124384791)
XLA Ops:
  1.3 0.3 fusion.1
  1.6 0.8 pad_maximum_fusion.2
  2.4 1.9 fusion
  4.3 1.3 pad_maximum_fusion
  5.6 701.6 %attend_and_hand.1 = (bf16[1,128,512]{2,1,0:T(8,128)(2,1)}, bf16[32,16,2048]{2,1,0:T(8,128)(2,1)}) custom-call(bf16[128,8192]{1,0:T(8,128)(2,1)} %bitcast.12, bf16[64,16,2048]{2,1,0:T(8,128)(2,1)} %bitcast.11, bf16[128,512]{1,0:T(8,128)(2,1)} %bitcast.13, bf16[512,2048]{1,0:T(8,128)(2,1)} %w_hbm.1, f32[1,1024]{1,0:T(1,128)} %bitcast.14, ...), custom_call_target="tpu_custom_call" | custom-call | flops 4499999744 | bytes 12000000 | tf_op jit(solution)/shard_map/attend_and_hand/pallas_call | solution.py:456
  707.3 1.6 copy.13
  708.8 3.2 copy.14
  (3 shorter events, 0.0 us)

commit v2 on v1

--- a/solution.py
+++ b/solution.py
@@ -25,6 +25,9 @@
 CHUNK = 4
 CHUNKS = 2 * QUARTERS * FIN // CHUNK
 WINDOW = 4
+SKEW = 2
+PER_UNIT = 1
+UNITS = 2 * KVH
 
 ROPE_BASE = 500000.0
 NEG_FILL = -1e30
@@ -66,6 +69,10 @@
     total = sum(p[1] * f for p, f in zip(parts, factors))
     numerator = sum(p[2] * f for p, f in zip(parts, factors))
     return top, total, numerator
+
+
+def steps_for(part):
+    return (part + 1) * CHUNKS // QUARTERS + SKEW * (NX - 1)
 
 
 def kernel(
@@ -194,13 +201,24 @@
             stream.at[d, n], stream.at[d, n], stream_send.at[d, n], stream_recv.at[d, n], at(x, onward, 1)
         )
 
-    def stream_step(n):
+    def stream_step(step):
         for d in range(2):
-            stream_copy(d, n).wait_recv()
-
-            @pl.when((z < NX - 1) if d == 0 else (z > 0))
+            n = step - SKEW * (z if d == 0 else NX - 1 - z)
+
+            @pl.when((n >= 0) & (n < CHUNKS))
             def _():
-                stream_copy(d, n).start()
+                stream_copy(d, n).wait_recv()
+
+                @pl.when((z < NX - 1) if d == 0 else (z > 0))
+                def _():
+                    stream_copy(d, n).start()
+
+    def stream_until(part, begun):
+        @pl.loop(begun, steps_for(part))
+        def _(step):
+            stream_step(step)
+
+        dispatch(part)
 
     def picked_copy(part, o):
         xx = plus(x, o)
@@ -258,7 +276,7 @@
             remote(xst.at[xx], xrt.at[o], xt_send.at[o], xt_recv.at[o], at(xx, z)),
         )
 
-    @pl.loop(0, 2 * KVH)
+    @pl.loop(0, UNITS)
     def _(u):
         j, half = lax.div(u, 2), lax.rem(u, 2)
         o = plus(lax.div(j, 2), 1)
@@ -306,13 +324,14 @@
 
         @pl.when(sec == 1)
         def _():
-            stream_step(u)
+            for i in range(PER_UNIT):
+                stream_step(u * PER_UNIT + i)
 
         @pl.when(u == 8)
         def _():
             fresh_sum_x()
 
-        @pl.when((sec == 1) & (u == 9))
+        @pl.when((sec == 1) & ((u + 1) * PER_UNIT == steps_for(0)))
         def _():
             for zz in range(NX):
                 remote(meta_out, meta_in.at[zz], meta_send.at[zz], meta_recv.at[zz], at(x, zz, 0)).wait_recv()
@@ -331,7 +350,7 @@
 
     @pl.when(sec == 1)
     def _():
-        dispatch(1)
+        stream_until(1, UNITS * PER_UNIT)
 
     for o in range(1, NX):
         for copy in xs_copy(o):
@@ -385,11 +404,7 @@
 
     @pl.when(sec == 1)
     def _():
-        @pl.loop(16, 24)
-        def _(n):
-            stream_step(n)
-
-        dispatch(2)
+        stream_until(2, steps_for(1))
 
     for o in range(1, NX):
         for copy in zs_copy(plus(z, o)):
@@ -404,11 +419,7 @@
 
     @pl.when(sec == 1)
     def _():
-        @pl.loop(24, 32)
-        def _(n):
-            stream_step(n)
-
-        dispatch(3)
+        stream_until(3, steps_for(2))
 
     for o in range(1, NX):
         for copy in xs_copy(o):

time: 722 us -> 136 us (0.19); the launches traced: 712 us -> 135 us
  Pallas kernels: 702 us -> 125 us
    pallas_call x1, Pallas kernels: 702 us -> 125 us  [shards(): pl.pallas_call(kernel, out_shape=(jax.ShapeDtypeStruct((1, ROWS, 512), BF...]
where the time goes in v2:
time: 136 us; the launch traced here: 135 us
  Pallas kernels  125 us (92%)
  local copies, waits for them, and re-layouts  4.73 us (3%)
  other arithmetic  4.29 us (3%)
    pallas_call x1, Pallas kernels, shards(): pl.pallas_call(kernel, out_shape=(jax.ShapeDtypeStruct((1, ROWS, 512), BF...  125 us
    unnamed x2, local copies, waits for them, and re-layouts  4.73 us

profile of v2, /device:TPU:240, one launch (start us, length us, event | category | flops | bytes accessed | tf_op | source)
XLA Modules:
  0.0 135.1 jit_solution(3259667845875731173)
XLA Ops:
  1.3 0.3 fusion.1
  1.6 0.8 pad_maximum_fusion.2
  2.4 1.9 %fusion = (f32[1024,64]{1,0:T(8,128)S(1)}, f32[1024,64]{1,0:T(8,128)S(1)}, f32[1024,64]{1,0:T(8,128)S(1)}) fusion(f32[64]{0:T(128)S(1)} %multiply_exponential_fusion, f32[1024]{0:T(1024)S(1)} %add_convert_fusion), kind=kLoop, calls=%fused_computation.4 | loop fusion | flops 131072 | bytes 790784 | tf_op jit(solution)/shard_map/neg | solution.py:47
  4.3 1.3 pad_maximum_fusion
  5.6 124.7 %attend_and_hand.1 = (bf16[1,128,512]{2,1,0:T(8,128)(2,1)}, bf16[32,16,2048]{2,1,0:T(8,128)(2,1)}) custom-call(bf16[128,8192]{1,0:T(8,128)(2,1)} %bitcast.12, bf16[64,16,2048]{2,1,0:T(8,128)(2,1)} %bitcast.11, bf16[128,512]{1,0:T(8,128)(2,1)} %bitcast.13, bf16[512,2048]{1,0:T(8,128)(2,1)} %w_hbm.1, f32[1,1024]{1,0:T(1,128)} %bitcast.14, ...), custom_call_target="tpu_custom_call" | custom-call | flops 4499999744 | bytes 12000000 | tf_op jit(solution)/shard_map/attend_and_hand/pallas_call | solution.py:467
  130.3 1.6 %copy.13 = bf16[1,128,512]{2,1,0:T(8,128)(2,1)} copy(bf16[1,128,512]{2,1,0:T(8,128)(2,1)} %get-tuple-element.18) | data formatting | bytes 262144
  131.9 3.2 %copy.14 = bf16[1,32,16,2048]{3,2,1,0:T(8,128)(2,1)} copy(bf16[1,32,16,2048]{3,2,1,0:T(8,128)(2,1)} %bitcast.10) | data formatting | bytes 4194304
  (3 shorter events, 0.0 us)

commit v3 on v1

v3 whole, which is shorter than its diff:
```python
import functools
import math

import jax
import jax.numpy as jnp
from jax import lax
from jax.experimental import pallas as pl
from jax.experimental.pallas import tpu as pltpu
from jax.sharding import PartitionSpec as P

HEADS = 64
KVH = 8
HD = 128
ROWS = 128
CTX = 1024
PAGE = 16
GQ = 8
KVW = 1024
PAGES = CTX // PAGE
FIN = 16
CAP = 2
NX = 4
RANKS = NX * NX
PARTS = 8
PCOLS = 2 * KVW // PARTS
WINDOW = 2
UNITS = KVH
WIDE = 512
SPAN = 64
BLOCKS = GQ * ROWS // WIDE
SEND_AT = ((1, 2), (2, 3), (4, 4), (5, 5), (6, 6), (7, 7))
DISPATCH_AT = ((3, 0), (5, 1), (7, 2))
FRESH_AT = 4

ROPE_BASE = 500000.0
NEG_FILL = -1e30
TO_LOG2 = math.log2(math.e) / math.sqrt(HD)

F32 = jnp.float32
BF16 = jnp.bfloat16
MESH = pl.DeviceIdType.MESH


def rope_tables(positions):
    half_width = HD // 2
    steps_index = jnp.arange(half_width, dtype=jnp.float32)
    inverse = jnp.exp(steps_index * (-2.0 * math.log(ROPE_BASE) / HD))
    angles = positions.astype(jnp.float32)[:, None] * inverse[None, :]
    return jnp.cos(angles), jnp.sin(angles)


def rotate(values, cosine, sine):
    swapped = pltpu.roll(values, HD // 2, 1)
    return values * cosine + swapped * sine


def dot_nt(a, b):
    return lax.dot_general(a, b, (((1,), (1,)), ((), ())), preferred_element_type=F32)


def soft_block(scores):
    peak = jnp.max(scores, axis=0, keepdims=True)
    weights = jnp.exp2(scores * TO_LOG2 - peak * TO_LOG2)
    total = jnp.sum(weights, axis=0, keepdims=True)
    return peak * TO_LOG2, total, weights.astype(BF16)


def merge(parts):
    top = functools.reduce(jnp.maximum, [p[0] for p in parts])
    factors = [jnp.exp2(p[0] - top) for p in parts]
    total = sum(p[1] * f for p, f in zip(parts, factors))
    numerator = sum(p[2] * f for p, f in zip(parts, factors))
    return top, total, numerator


def kernel(
    q_hbm, cache_hbm, fin_hbm, w_hbm, scale_ref, cos_half, sin_half, len_ref, plist_ref, own_ref,
    att_ref, handed_ref,
    q_ref, cache_ref, fin_ref, w_ref,
    keys, rows, vals_t, scores, weights, cos_ref, sin_ref,
    xs, xst, xr, xrt, zs, zst, zr, zrt,
    fs, fr, gs, gr,
    page_out, landed, work, picked, meta_out, meta_in, meta,
    load_sem, meta_send, meta_recv, meta_load, page_send, page_recv,
    xs_send, xs_recv, xt_send, xt_recv, zs_send, zs_recv, zt_send, zt_recv,
    f_send, f_recv, g_send, g_recv, pick_send, pick_recv, own_sem,
):
    sec, grp, rank = lax.axis_index("sec"), lax.axis_index("grp"), lax.axis_index("rank")
    x, z = lax.div(rank, NX), lax.rem(rank, NX)

    def at(xx, zz, section=None):
        return (sec if section is None else section, grp, xx * NX + zz)

    def remote(src, dst, send, recv, device):
        return pltpu.make_async_remote_copy(
            src_ref=src, dst_ref=dst, send_sem=send, recv_sem=recv, device_id=device, device_id_type=MESH
        )

    def plus(value, by):
        return lax.rem(value + by, NX)

    loads = [
        pltpu.make_async_copy(src, dst, load_sem.at[i])
        for i, (src, dst) in enumerate(
            ((cache_hbm, cache_ref), (fin_hbm, fin_ref), (w_hbm, w_ref), (q_hbm, q_ref))
        )
    ]
    for load in loads:
        load.start()

    barrier = pltpu.get_barrier_semaphore()
    for o in range(1, RANKS):
        peer = lax.rem(rank + o, RANKS)
        pl.semaphore_signal(barrier, inc=1, device_id=(sec, grp, peer), device_id_type=MESH)
    pl.semaphore_signal(barrier, inc=1, device_id=at(x, NX - 1 - z, 1 - sec), device_id_type=MESH)

    def page_copy(part):
        return remote(
            page_out.at[part], landed.at[part], page_send.at[part], page_recv.at[part], at(x, NX - 1 - z, 1)
        )

    def meta_copy():
        return remote(meta_out, meta_in, meta_send, meta_recv, at(x, NX - 1 - z, 1))

    loads[0].wait()

    @pl.when(sec == 0)
    def _():
        lanes = lax.broadcasted_iota(jnp.int32, (8, 128), 1)
        owner_of, slot_of = lanes // CAP, lanes % CAP
        count = jnp.zeros((8, 128), jnp.int32)
        chosen = jnp.full((8, 128), FIN, jnp.int32)
        for f in range(FIN):
            mine = owner_of == own_ref[f]
            chosen = jnp.where(mine & (count == slot_of), f, chosen)
            count = count + jnp.where(mine, 1, 0)
        meta_out[...] = chosen

        @pl.loop(0, FIN)
        def _(f):
            page = plist_ref[f]
            for part in range(PARTS):
                page_out[part, f] = cache_ref[page, :, part * PCOLS : (part + 1) * PCOLS]

    pl.semaphore_wait(barrier, RANKS)

    @pl.when(sec == 0)
    def _():
        meta_copy().start()
        for part in range(WINDOW):
            page_copy(part).start()

    loads[1].wait()
    loads[2].wait()

    def fresh_x(xx):
        o = plus(xx - x + NX, 0)
        return remote(fs.at[xx], fr.at[o], f_send.at[o], f_recv.at[o], at(xx, z))

    for xx in range(NX):
        for kind in range(2):
            cols = slice(kind * KVW + xx * 2 * HD, kind * KVW + (xx + 1) * 2 * HD)
            fs[xx, kind] = jnp.dot(fin_ref[...], w_ref[:, cols], preferred_element_type=F32)

        @pl.when(xx != x)
        def _():
            fresh_x(xx).start()

    def fresh_z(zz):
        o = plus(zz - z + NX, 0)
        return remote(gs.at[zz // 2], gr.at[o], g_send.at[o], g_recv.at[o], at(x, zz))

    def fresh_sum_x():
        for o in range(1, NX):
            remote(fs.at[0], fr.at[o], f_send.at[o], f_recv.at[o], at(plus(x, o), z)).wait_recv()
        for kind in range(2):
            total = fs[x, kind] + fr[1, kind] + fr[2, kind] + fr[3, kind]
            gs[0, kind] = total[:, :HD]
            gs[1, kind] = total[:, HD:]
        for zz in range(NX):

            @pl.when(zz != z)
            def _():
                fresh_z(zz).start()

    source = x * NX + NX - 1 - z

    def picked_copy(part, o):
        owner = lax.rem(rank + o, RANKS)
        return remote(
            picked.at[part, pl.ds(owner * CAP, CAP)],
            handed_ref.at[pl.ds(source * CAP, CAP), :, pl.ds(part * PCOLS, PCOLS)],
            pick_send.at[part, o],
            pick_recv.at[part, o],
            (1, grp, owner),
        )

    def picked_own(part):
        return pltpu.make_async_copy(
            picked.at[part, pl.ds(rank * CAP, CAP)],
            handed_ref.at[pl.ds(source * CAP, CAP), :, pl.ds(part * PCOLS, PCOLS)],
            own_sem.at[part],
        )

    def dispatch(part):
        if part == 0:
            meta_copy().wait_recv()
            load = pltpu.make_async_copy(meta_in, meta, meta_load)
            load.start()
            load.wait()
        page_copy(part).wait_recv()
        work[:FIN] = landed[part]
        for owner in range(RANKS):
            for c in range(CAP):
                picked[part, owner * CAP + c] = work[meta[0, owner * CAP + c]]

        @pl.loop(1, RANKS)
        def _(o):
            picked_copy(part, o).start()

        picked_own(part).start()

    def in_decode(*parts):
        @pl.when(sec == 1)
        def _():
            for part in parts:
                dispatch(part)

    @pl.when(sec == 1)
    def _():
        work[FIN] = jnp.zeros((PAGE, PCOLS), BF16)

    cos_ref[...] = jnp.concatenate([cos_half[...], cos_half[...]], axis=1)
    sin_ref[...] = jnp.concatenate([-sin_half[...], sin_half[...]], axis=1)
    loads[3].wait()
    edge = len_ref[0] - rank * CTX
    inside = lax.broadcasted_iota(jnp.int32, (CTX, HD), 0) < edge
    first = lax.broadcasted_iota(jnp.int32, (CTX, HD), 1) == 0
    keys[:, HD:] = jnp.where(first & jnp.logical_not(inside), NEG_FILL, 0.0).astype(BF16)
    rows[:, HD:] = jnp.where(first, 1.0, 0.0).astype(BF16)

    def xs_copy(o):
        xx = plus(x, o)
        return (
            remote(xs.at[xx], xr.at[o], xs_send.at[o], xs_recv.at[o], at(xx, z)),
            remote(xst.at[xx], xrt.at[o], xt_send.at[o], xt_recv.at[o], at(xx, z)),
        )

    @pl.loop(0, UNITS)
    def _(u):
        o = plus(lax.div(u, 2), 1)
        xx, hh = plus(x, o), lax.rem(u, 2)
        head = xx * 2 + hh
        cols = pl.ds(pl.multiple_of(head * HD, HD), HD)
        val_cols = pl.ds(pl.multiple_of(KVW + head * HD, HD), HD)
        for c in range(CTX // 128):
            span, pages = slice(c * 128, (c + 1) * 128), slice(c * 8, (c + 1) * 8)
            raw = cache_ref[pages, :, cols].reshape(128, HD).astype(F32) * scale_ref[:, cols]
            keys[span, :HD] = rotate(raw, cos_ref[span, :], sin_ref[span, :]).astype(BF16)
            vals_t[:, span] = cache_ref[pages, :, val_cols].reshape(128, HD).T
        for g in range(GQ):
            q_cols = pl.ds(pl.multiple_of((head * GQ + g) * HD, HD), HD)
            rows[g * ROWS : (g + 1) * ROWS, :HD] = rotate(
                q_ref[:, q_cols].astype(F32), cos_ref[CTX:, :], sin_ref[CTX:, :]
            ).astype(BF16)

        def score(b):
            scores[b] = dot_nt(keys[...], rows[b * WIDE : (b + 1) * WIDE, :])

        def weigh(b):
            peaks = scores[b, :SPAN].reshape(SPAN // 8, 8, WIDE).max(axis=0)
            for c in range(1, CTX // SPAN):
                part = scores[b, c * SPAN : (c + 1) * SPAN].reshape(SPAN // 8, 8, WIDE)
                peaks = jnp.maximum(peaks, part.max(axis=0))
            peak = peaks.max(axis=0, keepdims=True) * TO_LOG2
            base = jnp.broadcast_to(peak, (8, WIDE))
            totals = jnp.zeros((8, WIDE), F32)
            for c in range(CTX // SPAN):
                part = scores[b, c * SPAN : (c + 1) * SPAN].reshape(SPAN // 8, 8, WIDE)
                grown = jnp.exp2(part * TO_LOG2 - base[None])
                totals = totals + grown.sum(axis=0)
                weights[b, c * SPAN : (c + 1) * SPAN] = grown.reshape(SPAN, WIDE).astype(BF16)
            return peak, totals.sum(axis=0, keepdims=True)

        def add_up(b):
            numerator = jnp.dot(vals_t[...], weights[b], preferred_element_type=F32)
            xs[xx, hh, :, b * WIDE : (b + 1) * WIDE] = numerator.astype(BF16)

        stats = []
        score(0)
        for b in range(BLOCKS):
            if b + 1 < BLOCKS:
                score(b + 1)
            if b > 0:
                add_up(b - 1)
            stats.append(weigh(b))
        add_up(BLOCKS - 1)
        for h in range(2):

            @pl.when(hh == h)
            def _():
                for b in range(BLOCKS):
                    for i in range(2):
                        row = 2 * h + i
                        xst[xx, row : row + 1, b * WIDE : (b + 1) * WIDE] = stats[b][i]

        @pl.when((hh == 1) & (o != 0))
        def _():
            for copy in xs_copy(o):
                copy.start()

        for unit, part in SEND_AT:

            @pl.when((sec == 0) & (u == unit))
            def _():
                page_copy(part - WINDOW).wait_send()
                page_copy(part).start()

        for unit, part in DISPATCH_AT:

            @pl.when((sec == 1) & (u == unit))
            def _():
                dispatch(part)

        @pl.when(u == FRESH_AT)
        def _():
            fresh_sum_x()

    @pl.when(sec == 0)
    def _():
        picked[0] = jnp.zeros((RANKS * CAP, PAGE, PCOLS), BF16)
        for part in range(PARTS):
            pltpu.make_async_copy(
                picked.at[0], handed_ref.at[:, :, pl.ds(part * PCOLS, PCOLS)], own_sem.at[part]
            ).start()

    in_decode(3)

    for o in range(1, NX):
        for copy in xs_copy(o):
            copy.wait_recv()

    def zs_copy(zz):
        o = plus(zz - z + NX, 0)
        return (
            remote(zs.at[zz], zr.at[o], zs_send.at[o], zs_recv.at[o], at(x, zz)),
            remote(zst.at[zz], zrt.at[o], zt_send.at[o], zt_recv.at[o], at(x, zz)),
        )

    for zz in range(NX):
        hh, cols = zz // 2, slice((zz % 2) * 512, (zz % 2 + 1) * 512)
        parts = [
            (xst[x, 2 * hh : 2 * hh + 1, cols], xst[x, 2 * hh + 1 : 2 * hh + 2, cols], xs[x, hh, :, cols].astype(F32))
        ]
        for o in range(1, NX):
            parts.append(
                (
                    xrt[o, 2 * hh : 2 * hh + 1, cols],
                    xrt[o, 2 * hh + 1 : 2 * hh + 2, cols],
                    xr[o, hh, :, cols].astype(F32),
                )
            )
        top, total, numerator = merge(parts)
        zs[zz] = numerator.astype(BF16)
        zst[zz, 0:1, :] = top
        zst[zz, 1:2, :] = total

        @pl.when(zz != z)
        def _():
            for copy in zs_copy(zz):
                copy.start()

    in_decode(4, 5)

    for o in range(1, NX):
        remote(gs.at[0], gr.at[o], g_send.at[o], g_recv.at[o], at(x, plus(z, o))).wait_recv()
    mine = lax.div(z, 2)
    fresh = [(gs[mine, kind] + gr[1, kind] + gr[2, kind] + gr[3, kind]).astype(BF16) for kind in range(2)]
    fresh_keys = rotate(fresh[0].astype(F32), cos_ref[CTX:, :], sin_ref[CTX:, :]).astype(BF16)
    own_rows = []
    for h in range(HEADS // (NX * NX)):
        q_cols = pl.ds(pl.multiple_of((rank * 4 + h) * HD, HD), HD)
        own_rows.append(rotate(q_ref[:, q_cols].astype(F32), cos_ref[CTX:, :], sin_ref[CTX:, :]).astype(BF16))
    fresh_scores = dot_nt(fresh_keys, jnp.concatenate(own_rows, axis=0))
    key_row = lax.broadcasted_iota(jnp.int32, fresh_scores.shape, 0)
    query_row = lax.broadcasted_iota(jnp.int32, fresh_scores.shape, 1) % ROWS
    peak, total, fresh_weights = soft_block(jnp.where(key_row <= query_row, fresh_scores, NEG_FILL))
    numerator = jnp.dot(fresh[1].astype(F32).T.astype(BF16), fresh_weights, preferred_element_type=F32)
    parts = [(peak, total, numerator)]

    for o in range(1, NX):
        for copy in zs_copy(plus(z, o)):
            copy.wait_recv()
    parts.append((zst[z, 0:1, :], zst[z, 1:2, :], zs[z].astype(F32)))
    for o in range(1, NX):
        parts.append((zrt[o, 0:1, :], zrt[o, 1:2, :], zr[o].astype(F32)))
    _, total, numerator = merge(parts)
    result = numerator / total
    for h in range(HEADS // (NX * NX)):
        att_ref[0, :, h * HD : (h + 1) * HD] = result[:, h * ROWS : (h + 1) * ROWS].T.astype(BF16)

    in_decode(6, 7)

    for o in range(1, NX):
        for copy in xs_copy(o):
            copy.wait_send()
        for copy in zs_copy(plus(z, o)):
            copy.wait_send()
        fresh_x(plus(x, o)).wait_send()
        remote(gs.at[0], gr.at[o], g_send.at[o], g_recv.at[o], at(x, plus(z, o))).wait_send()

    @pl.when(sec == 0)
    def _():
        meta_copy().wait_send()
        for part in range(PARTS - WINDOW, PARTS):
            page_copy(part).wait_send()
        for part in range(PARTS):
            pltpu.make_async_copy(
                picked.at[0], handed_ref.at[:, :, pl.ds(part * PCOLS, PCOLS)], own_sem.at[part]
            ).wait()

    @pl.when(sec == 1)
    def _():
        for part in range(PARTS):

            @pl.loop(1, RANKS)
            def _(o):
                picked_copy(part, o).wait_send()
                picked_copy(part, o).wait_recv()

            picked_own(part).wait()


def shards(queries, kv_cache, key_scale, fresh_input, kv_weight, lengths, page_list, owners):
    position = lax.axis_index("rank")
    length = lengths[0, 0]
    places = jnp.arange(CTX + ROWS, dtype=jnp.int32)
    cosine, sine = rope_tables(jnp.where(places < CTX, position * CTX, length - CTX) + places)
    whole = pl.BlockSpec(memory_space=pltpu.VMEM)
    scalars = pl.BlockSpec(memory_space=pltpu.SMEM)
    anywhere = pl.BlockSpec(memory_space=pl.ANY)
    dma = pltpu.SemaphoreType.DMA
    attended, handed = pl.pallas_call(
        kernel,
        out_shape=(
            jax.ShapeDtypeStruct((1, ROWS, 512), BF16),
            jax.ShapeDtypeStruct((2 * FIN, PAGE, 2 * KVW), BF16),
        ),
        in_specs=[anywhere] * 4 + [whole] * 3 + [scalars] * 3,
        out_specs=(whole, anywhere),
        scratch_shapes=[
            pltpu.VMEM((ROWS, HEADS * HD), BF16),
            pltpu.VMEM((PAGES, PAGE, 2 * KVW), BF16),
            pltpu.VMEM((ROWS, 512), BF16),
            pltpu.VMEM((512, 2 * KVW), BF16),
            pltpu.VMEM((CTX, 2 * HD), BF16),
            pltpu.VMEM((CTX, 2 * HD), BF16),
            pltpu.VMEM((HD, CTX), BF16),
            pltpu.VMEM((BLOCKS, CTX, WIDE), F32),
            pltpu.VMEM((BLOCKS, CTX, WIDE), BF16),
            pltpu.VMEM((CTX + ROWS, HD), F32),
            pltpu.VMEM((CTX + ROWS, HD), F32),
            pltpu.VMEM((NX, 2, HD, CTX), BF16),
            pltpu.VMEM((NX, 8, CTX), F32),
            pltpu.VMEM((NX, 2, HD, CTX), BF16),
            pltpu.VMEM((NX, 8, CTX), F32),
            pltpu.VMEM((NX, HD, 512), BF16),
            pltpu.VMEM((NX, 8, 512), F32),
            pltpu.VMEM((NX, HD, 512), BF16),
            pltpu.VMEM((NX, 8, 512), F32),
            pltpu.VMEM((NX, 2, ROWS, 2 * HD), F32),
            pltpu.VMEM((NX, 2, ROWS, 2 * HD), F32),
            pltpu.VMEM((2, 2, ROWS, HD), F32),
            pltpu.VMEM((NX, 2, ROWS, HD), F32),
            pltpu.VMEM((PARTS, FIN, PAGE, PCOLS), BF16),
            pltpu.VMEM((PARTS, FIN, PAGE, PCOLS), BF16),
            pltpu.VMEM((FIN + 1, PAGE, PCOLS), BF16),
            pltpu.VMEM((PARTS, RANKS * CAP, PAGE, PCOLS), BF16),
            pltpu.VMEM((8, 128), jnp.int32),
            pltpu.VMEM((8, 128), jnp.int32),
            pltpu.SMEM((8, 128), jnp.int32),
            dma((4,)),
            dma,
            dma,
            dma,
            dma((PARTS,)),
            dma((PARTS,)),
        ]
        + [dma((NX,))] * 12
        + [dma((PARTS, RANKS)), dma((PARTS, RANKS)), dma((PARTS,))],
        compiler_params=pltpu.CompilerParams(
            collective_id=0, has_side_effects=True, vmem_limit_bytes=56 * 1024 * 1024
        ),
        cost_estimate=pl.CostEstimate(flops=4_500_000_000, bytes_accessed=12_000_000, transcendentals=8_500_000),
        name="attend_and_hand",
    )(
        queries[0],
        kv_cache.reshape(PAGES, PAGE, 2 * KVW),
        fresh_input[0],
        kv_weight,
        key_scale.reshape(1, KVW),
        cosine,
        sine,
        lengths.reshape(1),
        page_list,
        owners.reshape(FIN),
    )
    return attended, handed[None]


def solution(mesh):
    return jax.shard_map(
        shards,
        mesh=mesh,
        in_specs=(
            P(("sec", "grp"), None, None),
            P(("sec", "grp"), "rank", None),
            P(),
            P(("sec", "grp"), None, "rank"),
            P("rank", None),
            P(("sec", "grp"), None),
            P(("sec", "grp", "rank")),
            P(("sec", "grp", "rank"), None),
        ),
        out_specs=(P(("sec", "grp"), None, "rank"), P(("sec", "grp", "rank"), None, None, None)),
        check_vma=False,
    )
```

time: 722 us -> 106 us (0.15); the launches traced: 712 us -> 106 us
  Pallas kernels: 702 us -> 96.7 us
    pallas_call x1, Pallas kernels: 702 us -> 96.7 us  [shards(): pl.pallas_call(kernel, out_shape=(jax.ShapeDtypeStruct((1, ROWS, 512), BF...]
where the time goes in v3:
time: 106 us
  Pallas kernels  96.7 us (91%)
  local copies, waits for them, and re-layouts  4.73 us (4%)
  other arithmetic  3.26 us (3%)
  between operations  1.3 us (1%)
    pallas_call x1, Pallas kernels, shards(): pl.pallas_call(kernel, out_shape=(jax.ShapeDtypeStruct((1, ROWS, 512), BF...  96.7 us
    unnamed x2, local copies, waits for them, and re-layouts  4.73 us
    sin x1, other arithmetic, rope_tables(): return (jnp.cos(angles), jnp.sin(angles))  3.24 us

profile of v3, /device:TPU:240, one launch (start us, length us, event | category | flops | bytes accessed | tf_op | source)
XLA Modules:
  0.0 106.0 jit_solution(8925068494542550169)
XLA Ops:
  1.3 3.2 %multiply_sine_fusion = (f32[1152,64]{1,0:T(8,128)}, f32[1152,64]{1,0:T(8,128)}) fusion(f32[64]{0:T(128)S(1)} %multiply_exponential_fusion, f32[1152]{0:T(1024)S(1)} %add_convert_fusion), kind=kLoop, calls=%fused_computation | loop fusion | flops 73728 | bytes 594688 | tf_op jit(solution)/shard_map/sin | solution.py:49
  4.6 96.7 %attend_and_hand.1 = (bf16[1,128,512]{2,1,0:T(8,128)(2,1)}, bf16[32,16,2048]{2,1,0:T(8,128)(2,1)}) custom-call(bf16[128,8192]{1,0:T(8,128)(2,1)} %bitcast.11, bf16[64,16,2048]{2,1,0:T(8,128)(2,1)} %bitcast.10, bf16[128,512]{1,0:T(8,128)(2,1)} %bitcast.12, bf16[512,2048]{1,0:T(8,128)(2,1)} %w_hbm.1, f32[1,1024]{1,0:T(1,128)} %bitcast.13, ...), custom_call_target="tpu_custom_call" | custom-call | flops 4499999744 | bytes 12000000 | tf_op jit(solution)/shard_map/attend_and_hand/pallas_call | solution.py:443
  101.2 1.6 %copy.13 = bf16[1,128,512]{2,1,0:T(8,128)(2,1)} copy(bf16[1,128,512]{2,1,0:T(8,128)(2,1)} %get-tuple-element.10) | data formatting | bytes 262144
  102.8 3.2 %copy.14 = bf16[1,32,16,2048]{3,2,1,0:T(8,128)(2,1)} copy(bf16[1,32,16,2048]{3,2,1,0:T(8,128)(2,1)} %bitcast.9) | data formatting | bytes 4194304
  (2 shorter events, 0.0 us)

commit v4 on v3

--- a/solution.py
+++ b/solution.py
@@ -21,6 +21,7 @@
 CAP = 2
 NX = 4
 RANKS = NX * NX
+TABLE = CTX + ROWS
 PARTS = 8
 PCOLS = 2 * KVW // PARTS
 WINDOW = 2
@@ -29,8 +30,8 @@
 SPAN = 64
 BLOCKS = GQ * ROWS // WIDE
 SEND_AT = ((1, 2), (2, 3), (4, 4), (5, 5), (6, 6), (7, 7))
-DISPATCH_AT = ((3, 0), (5, 1), (7, 2))
-FRESH_AT = 4
+DISPATCH_AT = ((1,0),(3,1),(5,2),(7,3))
+FRESH_AT = 6
 
 ROPE_BASE = 500000.0
 NEG_FILL = -1e30
@@ -45,7 +46,7 @@
     half_width = HD // 2
     steps_index = jnp.arange(half_width, dtype=jnp.float32)
     inverse = jnp.exp(steps_index * (-2.0 * math.log(ROPE_BASE) / HD))
-    angles = positions.astype(jnp.float32)[:, None] * inverse[None, :]
+    angles = positions.astype(jnp.float32) * jnp.concatenate([inverse, inverse])[None, :]
     return jnp.cos(angles), jnp.sin(angles)
 
 
@@ -230,8 +231,13 @@
     def _():
         work[FIN] = jnp.zeros((PAGE, PCOLS), BF16)
 
-    cos_ref[...] = jnp.concatenate([cos_half[...], cos_half[...]], axis=1)
-    sin_ref[...] = jnp.concatenate([-sin_half[...], sin_half[...]], axis=1)
+    low = lax.broadcasted_iota(jnp.int32, (TABLE // 2, HD), 1) < HD // 2
+    cosine, sine = cos_half[...], sin_half[...]
+    cosine_swapped, sine_swapped = pltpu.roll(cosine, HD // 2, 1), pltpu.roll(sine, HD // 2, 1)
+    cos_ref[: TABLE // 2] = jnp.where(low, cosine, cosine_swapped)
+    cos_ref[TABLE // 2 :] = jnp.where(low, cosine_swapped, cosine)
+    sin_ref[: TABLE // 2] = jnp.where(low, -sine, sine_swapped)
+    sin_ref[TABLE // 2 :] = jnp.where(low, -sine_swapped, sine)
     loads[3].wait()
     edge = len_ref[0] - rank * CTX
     inside = lax.broadcasted_iota(jnp.int32, (CTX, HD), 0) < edge
@@ -334,7 +340,7 @@
                 picked.at[0], handed_ref.at[:, :, pl.ds(part * PCOLS, PCOLS)], own_sem.at[part]
             ).start()
 
-    in_decode(3)
+    in_decode(4, 5, 6)
 
     for o in range(1, NX):
         for copy in xs_copy(o):
@@ -370,7 +376,6 @@
             for copy in zs_copy(zz):
                 copy.start()
 
-    in_decode(4, 5)
 
     for o in range(1, NX):
         remote(gs.at[0], gr.at[o], g_send.at[o], g_recv.at[o], at(x, plus(z, o))).wait_recv()
@@ -388,6 +393,8 @@
     numerator = jnp.dot(fresh[1].astype(F32).T.astype(BF16), fresh_weights, preferred_element_type=F32)
     parts = [(peak, total, numerator)]
 
+    in_decode(7)
+
     for o in range(1, NX):
         for copy in zs_copy(plus(z, o)):
             copy.wait_recv()
@@ -399,8 +406,6 @@
     for h in range(HEADS // (NX * NX)):
         att_ref[0, :, h * HD : (h + 1) * HD] = result[:, h * ROWS : (h + 1) * ROWS].T.astype(BF16)
 
-    in_decode(6, 7)
-
     for o in range(1, NX):
         for copy in xs_copy(o):
             copy.wait_send()
@@ -431,10 +436,17 @@
             picked_own(part).wait()
 
 
+def place_kernel(att_in, handed_in, att_out, handed_out):
+    att_out[...] = att_in[...]
+    handed_out[0] = handed_in[...]
+
+
 def shards(queries, kv_cache, key_scale, fresh_input, kv_weight, lengths, page_list, owners):
     position = lax.axis_index("rank")
     length = lengths[0, 0]
-    places = jnp.arange(CTX + ROWS, dtype=jnp.int32)
+    places = lax.broadcasted_iota(jnp.int32, (TABLE // 2, HD), 0)
+    lanes = lax.broadcasted_iota(jnp.int32, (TABLE // 2, HD), 1)
+    places = places + jnp.where(lanes < HD // 2, 0, TABLE // 2)
     cosine, sine = rope_tables(jnp.where(places < CTX, position * CTX, length - CTX) + places)
     whole = pl.BlockSpec(memory_space=pltpu.VMEM)
     scalars = pl.BlockSpec(memory_space=pltpu.SMEM)
@@ -505,7 +517,18 @@
         page_list,
         owners.reshape(FIN),
     )
-    return attended, handed[None]
+    return pl.pallas_call(
+        place_kernel,
+        out_shape=(
+            jax.ShapeDtypeStruct((1, ROWS, 512), BF16),
+            jax.ShapeDtypeStruct((1, 2 * FIN, PAGE, 2 * KVW), BF16),
+        ),
+        in_specs=[whole] * 2,
+        out_specs=(whole, whole),
+
+        cost_estimate=pl.CostEstimate(flops=0, bytes_accessed=4_500_000, transcendentals=0),
+        name="place",
+    )(attended, handed)
 
 
 def solution(mesh):

time: 106 us -> 98.1 us (0.925)
  local copies, waits for them, and re-layouts: 4.73 us -> 0 us
  Pallas kernels: 96.7 us -> 94.7 us
  other arithmetic: 3.26 us -> 1.92 us
    pallas_call x1, Pallas kernels: 96.7 us -> 91.6 us  [shards(): pl.pallas_call(kernel, out_shape=(jax.ShapeDtypeStruct((1, ROWS, 512), BF...]
    unnamed x2 -> x0, local copies, waits for them, and re-layouts: 4.73 us -> none
    pallas_call x0 -> x1, Pallas kernels: none -> 3.13 us  [shards(): pl.pallas_call(place_kernel, out_shape=(jax.ShapeDtypeStruct((1, ROWS, 51...]
    sin x1, other arithmetic: 3.24 us -> 1.83 us  [rope_tables(): return (jnp.cos(angles), jnp.sin(angles))]
where the time goes in v4:
time: 98.1 us; the launch traced here: 97.9 us
  Pallas kernels  94.7 us (97%)
  other arithmetic  1.92 us (2%)
  between operations  1.29 us (1%)
    pallas_call x1, Pallas kernels, shards(): pl.pallas_call(kernel, out_shape=(jax.ShapeDtypeStruct((1, ROWS, 512), BF...  91.6 us
    pallas_call x1, Pallas kernels, shards(): pl.pallas_call(place_kernel, out_shape=(jax.ShapeDtypeStruct((1, ROWS, 51...  3.13 us

profile of v4, /device:TPU:240, one launch (start us, length us, event | category | flops | bytes accessed | tf_op | source)
XLA Modules:
  0.0 97.9 jit_solution(11699502185953263811)
XLA Ops:
  1.3 0.1 pad_maximum_fusion
  1.4 1.8 %fusion.1 = (f32[576,128]{1,0:T(8,128)}, f32[576,128]{1,0:T(8,128)}) fusion(f32[128]{0:T(128)S(1)} %pad_maximum_fusion, s32[]{:T(128)} %bitcast.4, s32[]{:T(128)S(6)} %mul.19, s32[128]{0:T(128)S(1)} %compare_select_fusion), kind=kLoop, calls=%fused_computation.3 | loop fusion | flops 442368 | bytes 590856 | tf_op jit(solution)/shard_map/sin | solution.py:50
  3.2 91.6 %attend_and_hand.1 = (bf16[1,128,512]{2,1,0:T(8,128)(2,1)}, bf16[32,16,2048]{2,1,0:T(8,128)(2,1)}) custom-call(bf16[128,8192]{1,0:T(8,128)(2,1)} %bitcast.9, bf16[64,16,2048]{2,1,0:T(8,128)(2,1)} %bitcast.8, bf16[128,512]{1,0:T(8,128)(2,1)} %bitcast.10, bf16[512,2048]{1,0:T(8,128)(2,1)} %w_hbm.1, f32[1,1024]{1,0:T(1,128)} %bitcast.11, ...), custom_call_target="tpu_custom_call" | custom-call | flops 4499999744 | bytes 12000000 | tf_op jit(solution)/shard_map/attend_and_hand/pallas_call | solution.py:455
  94.8 3.1 %place.1 = (bf16[1,128,512]{2,1,0:T(8,128)(2,1)}, bf16[1,32,16,2048]{3,2,1,0:T(8,128)(2,1)}) custom-call(bf16[1,128,512]{2,1,0:T(8,128)(2,1)} %get-tuple-element.4.att_in, bf16[32,16,2048]{2,1,0:T(8,128)(2,1)} %get-tuple-element.5.handed_in), custom_call_target="tpu_custom_call" | custom-call | bytes 4500000 | tf_op jit(solution)/shard_map/place/pallas_call | solution.py:520
  (2 shorter events, 0.0 us)

commit v5 on v4

--- a/solution.py
+++ b/solution.py
@@ -143,6 +143,26 @@
             for part in range(PARTS):
                 page_out[part, f] = cache_ref[page, :, part * PCOLS : (part + 1) * PCOLS]
 
+    loads[1].wait()
+    loads[2].wait()
+
+    def fresh_x(xx):
+        o = plus(xx - x + NX, 0)
+        return remote(fs.at[xx], fr.at[o], f_send.at[o], f_recv.at[o], at(xx, z))
+
+    for xx in range(NX):
+        for kind in range(2):
+            cols = slice(kind * KVW + xx * 2 * HD, kind * KVW + (xx + 1) * 2 * HD)
+            fs[xx, kind] = jnp.dot(fin_ref[...], w_ref[:, cols], preferred_element_type=F32)
+
+    low = lax.broadcasted_iota(jnp.int32, (TABLE // 2, HD), 1) < HD // 2
+    cosine, sine = cos_half[...], sin_half[...]
+    cosine_swapped, sine_swapped = pltpu.roll(cosine, HD // 2, 1), pltpu.roll(sine, HD // 2, 1)
+    cos_ref[: TABLE // 2] = jnp.where(low, cosine, cosine_swapped)
+    cos_ref[TABLE // 2 :] = jnp.where(low, cosine_swapped, cosine)
+    sin_ref[: TABLE // 2] = jnp.where(low, -sine, sine_swapped)
+    sin_ref[TABLE // 2 :] = jnp.where(low, -sine_swapped, sine)
+    loads[3].wait()
     pl.semaphore_wait(barrier, RANKS)
 
     @pl.when(sec == 0)
@@ -151,17 +171,7 @@
         for part in range(WINDOW):
             page_copy(part).start()
 
-    loads[1].wait()
-    loads[2].wait()
-
-    def fresh_x(xx):
-        o = plus(xx - x + NX, 0)
-        return remote(fs.at[xx], fr.at[o], f_send.at[o], f_recv.at[o], at(xx, z))
-
     for xx in range(NX):
-        for kind in range(2):
-            cols = slice(kind * KVW + xx * 2 * HD, kind * KVW + (xx + 1) * 2 * HD)
-            fs[xx, kind] = jnp.dot(fin_ref[...], w_ref[:, cols], preferred_element_type=F32)
 
         @pl.when(xx != x)
         def _():
@@ -231,14 +241,6 @@
     def _():
         work[FIN] = jnp.zeros((PAGE, PCOLS), BF16)
 
-    low = lax.broadcasted_iota(jnp.int32, (TABLE // 2, HD), 1) < HD // 2
-    cosine, sine = cos_half[...], sin_half[...]
-    cosine_swapped, sine_swapped = pltpu.roll(cosine, HD // 2, 1), pltpu.roll(sine, HD // 2, 1)
-    cos_ref[: TABLE // 2] = jnp.where(low, cosine, cosine_swapped)
-    cos_ref[TABLE // 2 :] = jnp.where(low, cosine_swapped, cosine)
-    sin_ref[: TABLE // 2] = jnp.where(low, -sine, sine_swapped)
-    sin_ref[TABLE // 2 :] = jnp.where(low, -sine_swapped, sine)
-    loads[3].wait()
     edge = len_ref[0] - rank * CTX
     inside = lax.broadcasted_iota(jnp.int32, (CTX, HD), 0) < edge
     first = lax.broadcasted_iota(jnp.int32, (CTX, HD), 1) == 0
@@ -340,7 +342,7 @@
                 picked.at[0], handed_ref.at[:, :, pl.ds(part * PCOLS, PCOLS)], own_sem.at[part]
             ).start()
 
-    in_decode(4, 5, 6)
+    in_decode(4, 5, 6, 7)
 
     for o in range(1, NX):
         for copy in xs_copy(o):
@@ -392,8 +394,6 @@
     peak, total, fresh_weights = soft_block(jnp.where(key_row <= query_row, fresh_scores, NEG_FILL))
     numerator = jnp.dot(fresh[1].astype(F32).T.astype(BF16), fresh_weights, preferred_element_type=F32)
     parts = [(peak, total, numerator)]
-
-    in_decode(7)
 
     for o in range(1, NX):
         for copy in zs_copy(plus(z, o)):
@@ -473,13 +473,13 @@
             pltpu.VMEM((CTX + ROWS, HD), F32),
             pltpu.VMEM((CTX + ROWS, HD), F32),
             pltpu.VMEM((NX, 2, HD, CTX), BF16),
-            pltpu.VMEM((NX, 8, CTX), F32),
+            pltpu.VMEM((NX, 4, CTX), F32),
             pltpu.VMEM((NX, 2, HD, CTX), BF16),
-            pltpu.VMEM((NX, 8, CTX), F32),
+            pltpu.VMEM((NX, 4, CTX), F32),
             pltpu.VMEM((NX, HD, 512), BF16),
-            pltpu.VMEM((NX, 8, 512), F32),
+            pltpu.VMEM((NX, 2, 512), F32),
             pltpu.VMEM((NX, HD, 512), BF16),
-            pltpu.VMEM((NX, 8, 512), F32),
+            pltpu.VMEM((NX, 2, 512), F32),
             pltpu.VMEM((NX, 2, ROWS, 2 * HD), F32),
             pltpu.VMEM((NX, 2, ROWS, 2 * HD), F32),
             pltpu.VMEM((2, 2, ROWS, HD), F32),

time: 98.1 us -> 94.8 us (0.966)
  Pallas kernels: 94.7 us -> 91.4 us
    pallas_call x1, Pallas kernels: 91.6 us -> 88.3 us  [shards(): pl.pallas_call(kernel, out_shape=(jax.ShapeDtypeStruct((1, ROWS, 512), BF...]
where the time goes in v5:
time: 94.8 us; the launch traced here: 94.7 us
  Pallas kernels  91.4 us (96%)
  other arithmetic  1.92 us (2%)
  between operations  1.29 us (1%)
    pallas_call x1, Pallas kernels, shards(): pl.pallas_call(kernel, out_shape=(jax.ShapeDtypeStruct((1, ROWS, 512), BF...  88.3 us
    pallas_call x1, Pallas kernels, shards(): pl.pallas_call(place_kernel, out_shape=(jax.ShapeDtypeStruct((1, ROWS, 51...  3.13 us

profile of v5, /device:TPU:240, one launch (start us, length us, event | category | flops | bytes accessed | tf_op | source)
XLA Modules:
  0.0 94.7 jit_solution(8708002822781729843)
XLA Ops:
  1.3 0.1 pad_maximum_fusion
  1.4 1.8 %fusion.1 = (f32[576,128]{1,0:T(8,128)}, f32[576,128]{1,0:T(8,128)}) fusion(f32[128]{0:T(128)S(1)} %pad_maximum_fusion, s32[]{:T(128)} %bitcast.4, s32[]{:T(128)S(6)} %mul.19, s32[128]{0:T(128)S(1)} %compare_select_fusion), kind=kLoop, calls=%fused_computation.3 | loop fusion | flops 442368 | bytes 590856 | tf_op jit(solution)/shard_map/sin | solution.py:50
  3.2 88.3 %attend_and_hand.1 = (bf16[1,128,512]{2,1,0:T(8,128)(2,1)}, bf16[32,16,2048]{2,1,0:T(8,128)(2,1)}) custom-call(bf16[128,8192]{1,0:T(8,128)(2,1)} %bitcast.9, bf16[64,16,2048]{2,1,0:T(8,128)(2,1)} %bitcast.8, bf16[128,512]{1,0:T(8,128)(2,1)} %bitcast.10, bf16[512,2048]{1,0:T(8,128)(2,1)} %w_hbm.1, f32[1,1024]{1,0:T(1,128)} %bitcast.11, ...), custom_call_target="tpu_custom_call" | custom-call | flops 4499999744 | bytes 12000000 | tf_op jit(solution)/shard_map/attend_and_hand/pallas_call | solution.py:455
  91.5 3.1 %place.1 = (bf16[1,128,512]{2,1,0:T(8,128)(2,1)}, bf16[1,32,16,2048]{3,2,1,0:T(8,128)(2,1)}) custom-call(bf16[1,128,512]{2,1,0:T(8,128)(2,1)} %get-tuple-element.4.att_in, bf16[32,16,2048]{2,1,0:T(8,128)(2,1)} %get-tuple-element.5.handed_in), custom_call_target="tpu_custom_call" | custom-call | bytes 4500000 | tf_op jit(solution)/shard_map/place/pallas_call | solution.py:520
  (2 shorter events, 0.0 us)

commit v6 on v5

--- a/solution.py
+++ b/solution.py
@@ -247,12 +247,16 @@
     keys[:, HD:] = jnp.where(first & jnp.logical_not(inside), NEG_FILL, 0.0).astype(BF16)
     rows[:, HD:] = jnp.where(first, 1.0, 0.0).astype(BF16)
 
+    def head_copy(o, h):
+        xx = plus(x, o)
+        return remote(xs.at[xx, h], xr.at[o, h], xs_send.at[o, h], xs_recv.at[o, h], at(xx, z))
+
+    def stat_copy(o):
+        xx = plus(x, o)
+        return remote(xst.at[xx], xrt.at[o], xt_send.at[o], xt_recv.at[o], at(xx, z))
+
     def xs_copy(o):
-        xx = plus(x, o)
-        return (
-            remote(xs.at[xx], xr.at[o], xs_send.at[o], xs_recv.at[o], at(xx, z)),
-            remote(xst.at[xx], xrt.at[o], xt_send.at[o], xt_recv.at[o], at(xx, z)),
-        )
+        return head_copy(o, 0), head_copy(o, 1), stat_copy(o)
 
     @pl.loop(0, UNITS)
     def _(u):
@@ -312,10 +316,13 @@
                         row = 2 * h + i
                         xst[xx, row : row + 1, b * WIDE : (b + 1) * WIDE] = stats[b][i]
 
+        @pl.when(o != 0)
+        def _():
+            head_copy(o, hh).start()
+
         @pl.when((hh == 1) & (o != 0))
         def _():
-            for copy in xs_copy(o):
-                copy.start()
+            stat_copy(o).start()
 
         for unit, part in SEND_AT:
 
@@ -498,7 +505,8 @@
             dma((PARTS,)),
             dma((PARTS,)),
         ]
-        + [dma((NX,))] * 12
+        + [dma((NX, 2))] * 2
+        + [dma((NX,))] * 10
         + [dma((PARTS, RANKS)), dma((PARTS, RANKS)), dma((PARTS,))],
         compiler_params=pltpu.CompilerParams(
             collective_id=0, has_side_effects=True, vmem_limit_bytes=56 * 1024 * 1024

time: 94.8 us -> 94.9 us (level)
  no operation moved by 1% of the time
where the time goes in v6:
time: 94.9 us; the launch traced here: 94.7 us
  Pallas kernels  91.5 us (96%)
  other arithmetic  1.92 us (2%)
  between operations  1.29 us (1%)
    pallas_call x1, Pallas kernels, shards(): pl.pallas_call(kernel, out_shape=(jax.ShapeDtypeStruct((1, ROWS, 512), BF...  88.4 us
    pallas_call x1, Pallas kernels, shards(): pl.pallas_call(place_kernel, out_shape=(jax.ShapeDtypeStruct((1, ROWS, 51...  3.13 us

profile of v6, /device:TPU:240, one launch (start us, length us, event | category | flops | bytes accessed | tf_op | source)
XLA Modules:
  0.0 94.7 jit_solution(16153687992975491904)
XLA Ops:
  1.3 0.1 pad_maximum_fusion
  1.4 1.8 %fusion.1 = (f32[576,128]{1,0:T(8,128)}, f32[576,128]{1,0:T(8,128)}) fusion(f32[128]{0:T(128)S(1)} %pad_maximum_fusion, s32[]{:T(128)} %bitcast.4, s32[]{:T(128)S(6)} %mul.19, s32[128]{0:T(128)S(1)} %compare_select_fusion), kind=kLoop, calls=%fused_computation.3 | loop fusion | flops 442368 | bytes 590856 | tf_op jit(solution)/shard_map/sin | solution.py:50
  3.2 88.4 %attend_and_hand.1 = (bf16[1,128,512]{2,1,0:T(8,128)(2,1)}, bf16[32,16,2048]{2,1,0:T(8,128)(2,1)}) custom-call(bf16[128,8192]{1,0:T(8,128)(2,1)} %bitcast.9, bf16[64,16,2048]{2,1,0:T(8,128)(2,1)} %bitcast.8, bf16[128,512]{1,0:T(8,128)(2,1)} %bitcast.10, bf16[512,2048]{1,0:T(8,128)(2,1)} %w_hbm.1, f32[1,1024]{1,0:T(1,128)} %bitcast.11, ...), custom_call_target="tpu_custom_call" | custom-call | flops 4499999744 | bytes 12000000 | tf_op jit(solution)/shard_map/attend_and_hand/pallas_call | solution.py:462
  91.6 3.1 %place.1 = (bf16[1,128,512]{2,1,0:T(8,128)(2,1)}, bf16[1,32,16,2048]{3,2,1,0:T(8,128)(2,1)}) custom-call(bf16[1,128,512]{2,1,0:T(8,128)(2,1)} %get-tuple-element.4.att_in, bf16[32,16,2048]{2,1,0:T(8,128)(2,1)} %get-tuple-element.5.handed_in), custom_call_target="tpu_custom_call" | custom-call | bytes 4500000 | tf_op jit(solution)/shard_map/place/pallas_call | solution.py:528
  (2 shorter events, 0.0 us)
